TPU v7x, 32 devices: a whole 2x2x4 slice. The times are simulated.
32 devices in a mesh: grp: 2 (over x), slab: 8 (over z, y), blk: 2 (over core).
Axes of the slice: x: 2, y: 2, z: 4, core: 2. Of those that a mesh axis runs over, the one named last changes fastest.
Arguments:
- volume: float32 [256, 8192], P(('grp', 'slab'), 'blk'), parts along dimension 0, may hold values from -6 to 6
- measured: float32 [6, 2048, 3072], P('grp', 'slab', 'blk'), parts along dimension 0, may hold values from -6 to 6
- band_start: int32 [3, 8], replicated, may hold values from 0 to 1536, as said below
- band_length: int32 [3, 8], replicated, may hold values from 257 to 512, as said below
- row_offset: int32 [3, 2, 128], replicated, may hold values from 0 to 511, as said below
- row_weight: float32 [3, 2, 128], replicated, may hold values from 0.2 to 1
- col_index: int32 [3, 2, 8192], replicated, may hold values from 0 to 3071, as said below
- col_weight: float32 [3, 2, 8192], replicated, may hold values from 0.2 to 1
Outputs:
- residual: float32 [6, 2048, 3072], P('grp', 'slab', 'blk'), parts along dimension 0
- gradient: float32 [256, 8192], P(('grp', 'slab'), 'blk'), parts along dimension 0
There are 2 independent parts, one for each index of `grp`. A program takes and returns all parts, laid end to end along the dimension named above; an argument that names none is the same for every part. Nothing has to cross between parts.
Inputs may be any that keep to these rules, and one draw needn't show every extreme that they name: Slab s's band in a view starts between (s - 1) * 256 and s * 256, and ends inside the panel: band_start + 512 <= 2048. `band_length`: at most 512, which some slab reaches in every view. `row_offset`: the taps of a slice are consecutive rows. `col_index`: the taps of a voxel column are consecutive columns.
All inputs are finite; a program needn't handle non-finite values.
Results may differ from a plain program's by a relative error of at most 0.0001.
Values sent between devices are 32-bit elements; how exact they have to be, the bound alone decides.
A program may use at most 128 MiB of HBM per device.

v0:
```python
import jax
import jax.numpy as jnp
from jax import lax
from jax.sharding import PartitionSpec as P

HIGH = lax.Precision.HIGHEST


def passed_along(x, axis, by):
    devices = lax.axis_size(axis)
    pairs = [(i, i + by) for i in range(devices) if 0 <= i + by < devices]
    return lax.ppermute(x, axis, pairs)


def with_halo(x, sides, width):
    for axis, dim in sides:
        devices, length = (lax.axis_size(axis), x.shape[dim])
        up = [(i, (i + 1) % devices) for i in range(devices - 1)]
        down = [(j, i) for i, j in up]
        last = lax.slice_in_dim(x, length - width, length, axis=dim)
        initial = lax.slice_in_dim(x, 0, width, axis=dim)
        before = lax.ppermute(last, axis, up)
        after = lax.ppermute(initial, axis, down)
        x = jnp.concatenate([before, x, after], axis=dim)
    return x


def band_matrix(offsets, tap_weights, band_rows):
    row_ids = lax.broadcasted_iota(jnp.int32, (band_rows, offsets.shape[1]), 0)
    hits = row_ids[None, :, :] == offsets[:, None, :]
    return jnp.sum(jnp.where(hits, tap_weights[:, None, :], 0.0), axis=0)


def project_band(slab_rows, columns, col_weights, offsets, tap_weights, band_rows, panel_cols):
    values = slab_rows[:, None, :] * col_weights[None, :, :]
    flattened = values.reshape(slab_rows.shape[0], -1)
    spread = (
        jnp.zeros((slab_rows.shape[0], panel_cols), jnp.float32)
        .at[:, columns.reshape(-1)]
        .add(flattened)
    )
    weights_band = band_matrix(offsets, tap_weights, band_rows)
    return jnp.dot(weights_band, spread, precision=HIGH, preferred_element_type=jnp.float32)


def spread_back(along_rows, columns, col_weights):
    picked = along_rows[:, columns]
    return jnp.sum(picked * col_weights[None, :, :], axis=1)


def back_band(window, columns, col_weights, offsets, tap_weights):
    weights_band = band_matrix(offsets, tap_weights, window.shape[0])
    along_rows = jnp.dot(weights_band.T, window, precision=HIGH, preferred_element_type=jnp.float32)
    return spread_back(along_rows, columns, col_weights)


def on_device(
    volume, measured, band_start, band_length, row_offset, row_weight, col_index, col_weight
):
    slab_id = lax.axis_index("slab")
    block_id = lax.axis_index("blk")
    block_count = lax.axis_size("blk")
    slab_depth, xy_cells = volume.shape
    view_count, owner_rows, part_cols = measured.shape
    panel_cols = part_cols * block_count
    band_rows = 2 * owner_rows
    frame_base = (slab_id - 1) * owner_rows
    my_columns = lax.dynamic_slice_in_dim(col_index, block_id * xy_cells, xy_cells, 2)
    my_col_weights = lax.dynamic_slice_in_dim(col_weight, block_id * xy_cells, xy_cells, 2)
    my_offsets = lax.dynamic_slice_in_dim(row_offset, slab_id * slab_depth, slab_depth, 2)
    my_tap_weights = lax.dynamic_slice_in_dim(row_weight, slab_id * slab_depth, slab_depth, 2)
    residuals = []
    gradient = jnp.zeros((slab_depth, xy_cells), jnp.float32)
    for view_id in range(view_count):
        first_row = lax.dynamic_index_in_dim(band_start[view_id], slab_id, 0, keepdims=False)
        live_rows = lax.dynamic_index_in_dim(band_length[view_id], slab_id, 0, keepdims=False)
        offsets = my_offsets[view_id]
        tap_weights = my_tap_weights[view_id]
        partial_value = project_band(
            volume,
            my_columns[view_id],
            my_col_weights[view_id],
            offsets,
            tap_weights,
            band_rows,
            panel_cols,
        )
        framed = lax.dynamic_update_slice_in_dim(
            jnp.zeros((3 * owner_rows, panel_cols), jnp.float32),
            partial_value,
            first_row - frame_base,
            0,
        )
        upward = passed_along(framed[:owner_rows], "slab", -1)
        downward = passed_along(framed[2 * owner_rows :], "slab", 1)
        projected = lax.psum_scatter(
            framed[owner_rows : 2 * owner_rows] + upward + downward,
            "blk",
            scatter_dimension=1,
            tiled=True,
        )
        residual = measured[view_id] - projected
        residuals.append(residual)
        wide_rows = lax.all_gather(residual, "blk", axis=1, tiled=True)
        full_frame = with_halo(wide_rows, (("slab", 0),), owner_rows)
        window = lax.dynamic_slice_in_dim(full_frame, first_row - frame_base, band_rows, 0)
        inside = lax.broadcasted_iota(jnp.int32, (band_rows, 1), 0) < live_rows
        window = jnp.where(inside, window, 0.0)
        gradient = gradient + back_band(
            window, my_columns[view_id], my_col_weights[view_id], offsets, tap_weights
        )
    return (jnp.stack(residuals), gradient * (1.0 / view_count))


def solution(mesh):
    return jax.shard_map(
        on_device,
        mesh=mesh,
        in_specs=(P(("grp", "slab"), "blk"), P("grp", "slab", "blk"), P(), P(), P(), P(), P(), P()),
        out_specs=(P("grp", "slab", "blk"), P(("grp", "slab"), "blk")),
        check_vma=False,
    )
```

profile of v0, /device:TPU:0, one launch (start us, length us, event | category | flops | bytes accessed | tf_op | source)
XLA Modules:
  0.0 1176.0 jit_solution(9579208295670711002)
XLA Ops:
  7.2 0.8 fusion.42
  8.0 0.8 fusion.41
  8.8 0.8 dynamic-slice_bitcast_fusion.2
  9.7 0.9 dynamic-slice_bitcast_fusion.6
  10.6 1.5 copy.19
  12.2 0.6 constant_dynamic-slice_fusion.6
  13.5 6.8 bitcast_multiply_fusion.2
  20.4 40.7 %scatter_custom_fusion = f32[16,3072]{0,1:T(8,128)S(1)} fusion(s32[8192]{0:T(1024)S(1)} %bitcast.117, f32[16,8192]{0,1:T(8,128)} %get-tuple-element.15, f32[]{:T(128)} %constant.43.clone.1), kind=kCustom, calls=%fused_computation.35 | custom fusion | flops 131072 | bytes 720900 | tf_op jit(solution)/shard_map/scatter-add | solution.py:40
  61.1 7.1 fusion.56
  68.2 4.8 broadcast.124.clone
  73.0 15.4 %dynamic_update_slice.9 = f32[768,3072]{1,0:T(8,128)} dynamic-update-slice(f32[768,3072]{1,0:T(8,128)} %broadcast.124.clone, f32[512,3072]{1,0:T(8,128)} %fusion.56, s32[]{:T(128)S(6)} %select_n.117, s32[]{:T(128)} %constant.44.clone.1) | dynamic-update-slice | bytes 12582916 | tf_op jit(solution)/shard_map/dynamic_update_slice | solution.py:88
  88.4 3.3 fusion.51
  91.7 5.2 collective-permute-start.1
  96.9 1.3 collective-permute-start
  98.3 133.2 %collective-permute-done.1 = f32[256,3072]{1,0:T(8,128)S(1)} collective-permute-done((f32[256,3072]{1,0:T(8,128)S(1)}, f32[256,3072]{1,0:T(8,128)S(1)}, u32[]{:S(2)}, u32[]{:S(2)}) %collective-permute-start.1) | collective-permute-done | bytes 3145760 | tf_op jit(solution)/shard_map/ppermute | solution.py:12
  231.5 4.3 fusion.23
  235.9 0.6 constant_dynamic-slice_fusion.7
  237.1 51.8 %scatter_custom_fusion.2 = f32[16,3072]{0,1:T(8,128)S(1)} fusion(s32[8192]{0:T(1024)S(1)} %bitcast.118, f32[16,8192]{0,1:T(8,128)} %get-tuple-element.16, f32[]{:T(128)} %constant.43.clone.1), kind=kCustom, calls=%fused_computation.31 | custom fusion | flops 131072 | bytes 720900 | tf_op jit(solution)/shard_map/scatter-add | solution.py:40
  289.0 7.1 fusion.58
  296.1 4.8 broadcast.124.clone.1
  300.9 15.4 %dynamic_update_slice.11 = f32[768,3072]{1,0:T(8,128)} dynamic-update-slice(f32[768,3072]{1,0:T(8,128)} %broadcast.124.clone.1, f32[512,3072]{1,0:T(8,128)} %fusion.58, s32[]{:T(128)S(6)} %select_n.123, s32[]{:T(128)} %constant.44.clone.1) | dynamic-update-slice | bytes 12582916 | tf_op jit(solution)/shard_map/dynamic_update_slice | solution.py:88
  316.3 3.3 fusion.53
  319.6 4.9 collective-permute-start.5
  324.5 1.3 collective-permute-start.4
  325.8 132.3 %collective-permute-done.5 = f32[256,3072]{1,0:T(8,128)S(1)} collective-permute-done((f32[256,3072]{1,0:T(8,128)S(1)}, f32[256,3072]{1,0:T(8,128)S(1)}, u32[]{:S(2)}, u32[]{:S(2)}) %collective-permute-start.5) | collective-permute-done | bytes 3145760 | tf_op jit(solution)/shard_map/ppermute | solution.py:12
  458.2 4.4 fusion.21
  463.3 40.7 %scatter_custom_fusion.1 = f32[16,3072]{0,1:T(8,128)S(1)} fusion(s32[8192]{0:T(1024)S(1)} %bitcast.119, f32[16,8192]{0,1:T(8,128)} %get-tuple-element.17, f32[]{:T(128)} %constant.43.clone.1), kind=kCustom, calls=%fused_computation.33 | custom fusion | flops 131072 | bytes 720900 | tf_op jit(solution)/shard_map/scatter-add | solution.py:40
  504.1 7.1 fusion.57
  511.2 4.8 broadcast.124.clone.2
  516.0 15.4 %dynamic_update_slice.10 = f32[768,3072]{1,0:T(8,128)} dynamic-update-slice(f32[768,3072]{1,0:T(8,128)} %broadcast.124.clone.2, f32[512,3072]{1,0:T(8,128)} %fusion.57, s32[]{:T(128)S(6)} %select_n.120, s32[]{:T(128)} %constant.44.clone.1) | dynamic-update-slice | bytes 12582916 | tf_op jit(solution)/shard_map/dynamic_update_slice | solution.py:88
  531.4 3.3 fusion.52
  534.6 4.9 collective-permute-start.3
  539.6 1.3 collective-permute-start.2
  540.9 131.5 %collective-permute-done.3 = f32[256,3072]{1,0:T(8,128)S(1)} collective-permute-done((f32[256,3072]{1,0:T(8,128)S(1)}, f32[256,3072]{1,0:T(8,128)S(1)}, u32[]{:S(2)}, u32[]{:S(2)}) %collective-permute-start.3) | collective-permute-done | bytes 3145760 | tf_op jit(solution)/shard_map/ppermute | solution.py:12
  672.3 4.3 fusion.22
  676.7 18.0 %reduce-scatter.6.cloned.1.call-done = f32[256,1536]{1,0:T(8,128)} async-done(((f32[256,3072]{1,0:T(8,128)}), f32[256,1536]{1,0:T(8,128)}) %reduce-scatter.6.cloned.1.call-update) | async-done | bytes 1572880 | tf_op jit(solution)/shard_map/reduce_scatter | solution.py:96
  694.8 6.2 bitcast_subtract_fusion.2
  702.1 12.3 %all-gather.8.cloned.1.call-done = f32[256,3072]{1,0:T(8,128)} async-done(((f32[256,1536]{1,0:T(8,128)}), f32[256,3072]{1,0:T(8,128)}) %all-gather.8.cloned.1.call-update) | async-done | bytes 3145744 | tf_op jit(solution)/shard_map/all_gather | solution.py:104
  714.4 5.3 collective-permute-start.10
  719.8 1.3 collective-permute-start.11
  721.0 8.7 all-gather.4.cloned.1.call-done
  729.8 5.3 collective-permute-start.6
  735.1 1.3 collective-permute-start.7
  736.4 8.2 all-gather.6.cloned.1.call-done
  744.6 5.3 collective-permute-start.8
  749.9 171.7 %collective-permute-done.10 = f32[256,3072]{1,0:T(8,128)} collective-permute-done((f32[256,3072]{1,0:T(8,128)}, f32[256,3072]{1,0:T(8,128)}, u32[]{:S(2)}, u32[]{:S(2)}) %collective-permute-start.10) | collective-permute-done | bytes 3145760 | tf_op jit(solution)/shard_map/ppermute | solution.py:22
  921.6 1.3 collective-permute-start.9
  923.0 0.6 constant_dynamic-slice_fusion.4
  923.7 0.6 iota_compare_fusion.3
  924.3 0.7 iota_compare_fusion.5
  925.0 0.6 iota_compare_fusion.4
  925.6 4.2 pad_maximum_fusion
  929.8 13.2 %fusion.3 = f32[16,3072]{0,1:T(8,128)S(1)} fusion(f32[512,16]{0,1:T(8,128)S(1)} %get-tuple-element.42, s32[]{:T(128)S(6)} %select_n.123, f32[256,3072]{1,0:T(8,128)} %collective-permute-done.10, f32[256,3072]{1,0:T(8,128)S(1)} %copy-done.9, f32[256,3072]{1,0:T(8,128)} %collective-permute-done.11, pred[512]{0:T(512)(128)(4,1)S(1)} %iota_compare_fusion.3), kind=kOutput, calls=%fused_computation.21 | convolution fusion | flops 306708480 | bytes 9667076 | tf_op jit(solution)/shard_map/dot_general | solution.py:53
  943.0 27.9 %gather_fusion.2 = f32[8192,16]{1,0:T(8,128)} fusion(f32[16,3072]{0,1:T(8,128)S(1)} %fusion.3, s32[8192]{0:T(1024)S(1)} %broadcast_clamp_fusion), kind=kCustom, calls=%fused_computation.2 | custom fusion | bytes 1081344 | tf_op jit(solution)/shard_map/gather | solution.py:47
  970.9 85.5 %collective-permute-done.6 = f32[256,3072]{1,0:T(8,128)} collective-permute-done((f32[256,3072]{1,0:T(8,128)}, f32[256,3072]{1,0:T(8,128)}, u32[]{:S(2)}, u32[]{:S(2)}) %collective-permute-start.6) | collective-permute-done | bytes 3145760 | tf_op jit(solution)/shard_map/ppermute | solution.py:22
  1056.4 13.2 %fusion.13 = f32[16,3072]{0,1:T(8,128)S(1)} fusion(f32[512,16]{0,1:T(8,128)S(1)} %select_reduce_fusion.2, s32[]{:T(128)S(6)} %select_n.117, f32[256,3072]{1,0:T(8,128)} %collective-permute-done.6, f32[256,3072]{1,0:T(8,128)} %all-gather.4.cloned.1.call-done, f32[256,3072]{1,0:T(8,128)} %collective-permute-done.7, pred[512]{0:T(512)(128)(4,1)S(1)} %iota_compare_fusion.5), kind=kOutput, calls=%fused_computation.29 | convolution fusion | flops 306708480 | bytes 9667076 | tf_op jit(solution)/shard_map/dot_general | solution.py:53
  1069.6 28.0 %gather_fusion = f32[8192,16]{1,0:T(8,128)} fusion(f32[16,3072]{0,1:T(8,128)S(1)} %fusion.13, s32[8192]{0:T(1024)S(1)} %broadcast_clamp_fusion.2), kind=kCustom, calls=%fused_computation | custom fusion | bytes 1081344 | tf_op jit(solution)/shard_map/gather | solution.py:47
  1097.7 4.4 multiply_reduce_fusion
  1102.1 4.4 multiply_reduce_fusion.2
  1106.5 16.7 %collective-permute-done.8 = f32[256,3072]{1,0:T(8,128)} collective-permute-done((f32[256,3072]{1,0:T(8,128)}, f32[256,3072]{1,0:T(8,128)}, u32[]{:S(2)}, u32[]{:S(2)}) %collective-permute-start.8) | collective-permute-done | bytes 3145760 | tf_op jit(solution)/shard_map/ppermute | solution.py:22
  1123.2 12.8 %fusion.8 = f32[16,3072]{0,1:T(8,128)S(1)} fusion(f32[512,16]{0,1:T(8,128)S(1)} %get-tuple-element.43, s32[]{:T(128)S(6)} %select_n.120, f32[256,3072]{1,0:T(8,128)} %collective-permute-done.8, f32[256,3072]{1,0:T(8,128)S(1)} %copy-done.8, f32[256,3072]{1,0:T(8,128)} %collective-permute-done.9, pred[512]{0:T(512)(128)(4,1)S(1)} %iota_compare_fusion.4), kind=kOutput, calls=%fused_computation.25 | convolution fusion | flops 306708480 | bytes 9667076 | tf_op jit(solution)/shard_map/dot_general | solution.py:53
  1136.0 27.9 %gather_fusion.1 = f32[8192,16]{1,0:T(8,128)} fusion(f32[16,3072]{0,1:T(8,128)S(1)} %fusion.8, s32[8192]{0:T(1024)S(1)} %broadcast_clamp_fusion.1), kind=kCustom, calls=%fused_computation.1 | custom fusion | bytes 1081344 | tf_op jit(solution)/shard_map/gather | solution.py:47
  1163.9 3.1 multiply_reduce_fusion.1
  1167.7 1.3 copy.23
  (61 shorter events, 2.6 us)
Async XLA Ops:
  7.2 5.0 copy-start.6
  7.2 5.0 copy-start.7
  7.2 669.5 %reduce-scatter.4.cloned.1.call-start = ((), (), s32[]{:S(2)}) async-start(), calls=%async_computation.3 | async-start | bytes 4718592 | tf_op jit(solution)/shard_map/reduce_scatter | solution.py:96
  91.7 139.8 %collective-permute-start.1 = (f32[256,3072]{1,0:T(8,128)S(1)}, f32[256,3072]{1,0:T(8,128)S(1)}, u32[]{:S(2)}, u32[]{:S(2)}) collective-permute-start(f32[256,3072]{1,0:T(8,128)S(1)} %get-tuple-element.7), channel_id=1, source_target_pairs={{0,2},{2,4},{4,6},{6,8},{8,10},{10,12},{12,14},{1,3},{3,5},{5,7},{... | collective-permute-start | bytes 9437192 | tf_op jit(solution)/shard_map/ppermute | solution.py:12
  96.9 134.6 %collective-permute-start = (f32[256,3072]{1,0:T(8,128)S(1)}, f32[256,3072]{1,0:T(8,128)S(1)}, u32[]{:S(2)}, u32[]{:S(2)}) collective-permute-start(f32[256,3072]{1,0:T(8,128)S(1)} %get-tuple-element.6), channel_id=1, source_target_pairs={{2,0},{4,2},{6,4},{8,6},{10,8},{12,10},{14,12},{3,1},{5,3},{7,5},{... | collective-permute-start | bytes 9437192 | tf_op jit(solution)/shard_map/ppermute | solution.py:12
  235.8 440.9 %reduce-scatter.8.cloned.1.call-start = ((), (), s32[]{:S(2)}) async-start(), calls=%async_computation.5 | async-start | bytes 4718592 | tf_op jit(solution)/shard_map/reduce_scatter | solution.py:96
  319.6 138.6 %collective-permute-start.5 = (f32[256,3072]{1,0:T(8,128)S(1)}, f32[256,3072]{1,0:T(8,128)S(1)}, u32[]{:S(2)}, u32[]{:S(2)}) collective-permute-start(f32[256,3072]{1,0:T(8,128)S(1)} %get-tuple-element.11), channel_id=1, source_target_pairs={{0,2},{2,4},{4,6},{6,8},{8,10},{10,12},{12,14},{1,3},{3,5},{5,7},{... | collective-permute-start | bytes 9437192 | tf_op jit(solution)/shard_map/ppermute | solution.py:12
  324.5 133.7 %collective-permute-start.4 = (f32[256,3072]{1,0:T(8,128)S(1)}, f32[256,3072]{1,0:T(8,128)S(1)}, u32[]{:S(2)}, u32[]{:S(2)}) collective-permute-start(f32[256,3072]{1,0:T(8,128)S(1)} %get-tuple-element.10), channel_id=1, source_target_pairs={{2,0},{4,2},{6,4},{8,6},{10,8},{12,10},{14,12},{3,1},{5,3},{7,5},{... | collective-permute-start | bytes 9437192 | tf_op jit(solution)/shard_map/ppermute | solution.py:12
  462.6 232.2 %reduce-scatter.6.cloned.1.call-start = ((), (), s32[]{:S(2)}) async-start(), calls=%async_computation.4 | async-start | bytes 4718592 | tf_op jit(solution)/shard_map/reduce_scatter | solution.py:96
  534.6 137.7 %collective-permute-start.3 = (f32[256,3072]{1,0:T(8,128)S(1)}, f32[256,3072]{1,0:T(8,128)S(1)}, u32[]{:S(2)}, u32[]{:S(2)}) collective-permute-start(f32[256,3072]{1,0:T(8,128)S(1)} %get-tuple-element.9), channel_id=1, source_target_pairs={{0,2},{2,4},{4,6},{6,8},{8,10},{10,12},{12,14},{1,3},{3,5},{5,7},{... | collective-permute-start | bytes 9437192 | tf_op jit(solution)/shard_map/ppermute | solution.py:12
  539.6 132.8 %collective-permute-start.2 = (f32[256,3072]{1,0:T(8,128)S(1)}, f32[256,3072]{1,0:T(8,128)S(1)}, u32[]{:S(2)}, u32[]{:S(2)}) collective-permute-start(f32[256,3072]{1,0:T(8,128)S(1)} %get-tuple-element.8), channel_id=1, source_target_pairs={{2,0},{4,2},{6,4},{8,6},{10,8},{12,10},{14,12},{3,1},{5,3},{7,5},{... | collective-permute-start | bytes 9437192 | tf_op jit(solution)/shard_map/ppermute | solution.py:12
  676.6 37.8 %all-gather.8.cloned.1.call-start = ((), (), s32[]{:S(2)}) async-start(), calls=%async_computation.8 | async-start | bytes 4718592 | tf_op jit(solution)/shard_map/all_gather | solution.py:104
  700.9 222.0 %copy-start.5 = (s32[3,2,8192]{2,1,0:T(2,128)S(1)}, s32[3,2,8192]{2,1,0:T(2,128)}, u32[]{:S(2)}) copy-start(s32[3,2,8192]{2,1,0:T(2,128)} %param.14) | copy-start | bytes 589828
  700.9 224.6 %copy-start = (f32[256,1536]{1,0:T(8,128)S(1)}, f32[256,1536]{1,0:T(8,128)}, u32[]{:S(2)}) copy-start(f32[256,1536]{1,0:T(8,128)} %get-tuple-element.12) | copy-start | bytes 4718596
  700.9 224.6 %copy-start.1 = (f32[256,1536]{1,0:T(8,128)S(1)}, f32[256,1536]{1,0:T(8,128)}, u32[]{:S(2)}) copy-start(f32[256,1536]{1,0:T(8,128)} %get-tuple-element.13) | copy-start | bytes 4718596
  701.0 28.8 %all-gather.4.cloned.1.call-start = ((), (), s32[]{:S(2)}) async-start(), calls=%async_computation.6 | async-start | bytes 4718592 | tf_op jit(solution)/shard_map/all_gather | solution.py:104
  701.6 43.0 %all-gather.6.cloned.1.call-start = ((), (), s32[]{:S(2)}) async-start(), calls=%async_computation.7 | async-start | bytes 4718592 | tf_op jit(solution)/shard_map/all_gather | solution.py:104
  714.4 207.2 %collective-permute-start.10 = (f32[256,3072]{1,0:T(8,128)}, f32[256,3072]{1,0:T(8,128)}, u32[]{:S(2)}, u32[]{:S(2)}) collective-permute-start(f32[256,3072]{1,0:T(8,128)} %all-gather.8.cloned.1.call-done), channel_id=1, source_target_pairs={{0,2},{2,4},{4,6},{6,8},{8,10},{10,12},{12,14},{1,3},{3,5},{5,7},{... | collective-permute-start | bytes 9437192 | tf_op jit(solution)/shard_map/ppermute | solution.py:22
  719.8 210.0 %collective-permute-start.11 = (f32[256,3072]{1,0:T(8,128)}, f32[256,3072]{1,0:T(8,128)}, u32[]{:S(2)}, u32[]{:S(2)}) collective-permute-start(f32[256,3072]{1,0:T(8,128)} %all-gather.8.cloned.1.call-done), channel_id=1, source_target_pairs={{2,0},{4,2},{6,4},{8,6},{10,8},{12,10},{14,12},{3,1},{5,3},{7,5},{... | collective-permute-start | bytes 9437192 | tf_op jit(solution)/shard_map/ppermute | solution.py:23
  729.8 326.7 %collective-permute-start.6 = (f32[256,3072]{1,0:T(8,128)}, f32[256,3072]{1,0:T(8,128)}, u32[]{:S(2)}, u32[]{:S(2)}) collective-permute-start(f32[256,3072]{1,0:T(8,128)} %all-gather.4.cloned.1.call-done), channel_id=1, source_target_pairs={{0,2},{2,4},{4,6},{6,8},{8,10},{10,12},{12,14},{1,3},{3,5},{5,7},{... | collective-permute-start | bytes 9437192 | tf_op jit(solution)/shard_map/ppermute | solution.py:22
  735.1 321.3 %collective-permute-start.7 = (f32[256,3072]{1,0:T(8,128)}, f32[256,3072]{1,0:T(8,128)}, u32[]{:S(2)}, u32[]{:S(2)}) collective-permute-start(f32[256,3072]{1,0:T(8,128)} %all-gather.4.cloned.1.call-done), channel_id=1, source_target_pairs={{2,0},{4,2},{6,4},{8,6},{10,8},{12,10},{14,12},{3,1},{5,3},{7,5},{... | collective-permute-start | bytes 9437192 | tf_op jit(solution)/shard_map/ppermute | solution.py:23
  744.6 378.7 %collective-permute-start.8 = (f32[256,3072]{1,0:T(8,128)}, f32[256,3072]{1,0:T(8,128)}, u32[]{:S(2)}, u32[]{:S(2)}) collective-permute-start(f32[256,3072]{1,0:T(8,128)} %all-gather.6.cloned.1.call-done), channel_id=1, source_target_pairs={{0,2},{2,4},{4,6},{6,8},{8,10},{10,12},{12,14},{1,3},{3,5},{5,7},{... | collective-permute-start | bytes 9437192 | tf_op jit(solution)/shard_map/ppermute | solution.py:22
  921.6 201.6 %collective-permute-start.9 = (f32[256,3072]{1,0:T(8,128)}, f32[256,3072]{1,0:T(8,128)}, u32[]{:S(2)}, u32[]{:S(2)}) collective-permute-start(f32[256,3072]{1,0:T(8,128)} %all-gather.6.cloned.1.call-done), channel_id=1, source_target_pairs={{2,0},{4,2},{6,4},{8,6},{10,8},{12,10},{14,12},{3,1},{5,3},{7,5},{... | collective-permute-start | bytes 9437192 | tf_op jit(solution)/shard_map/ppermute | solution.py:23
  925.6 4.2 copy-start.9
  1097.7 4.5 copy-start.4
  1102.1 21.1 %copy-start.8 = (f32[256,3072]{1,0:T(8,128)S(1)}, f32[256,3072]{1,0:T(8,128)}, u32[]{:S(2)}) copy-start(f32[256,3072]{1,0:T(8,128)} %all-gather.6.cloned.1.call-done) | copy-start | bytes 9437188
  1163.9 3.1 copy-start.2
  1163.9 3.5 copy-start.3
Sparse Core Ops, SparseCore 0:
  235.9 13.2 reduce-scatter.3
  462.7 15.1 reduce-scatter.7
  676.8 17.9 reduce-scatter.5
  701.1 13.2 all-gather.7
  716.4 13.2 all-gather.3
  731.2 13.2 all-gather.5
where the time goes:
time: 1180 us
  waiting for transfers between devices  719 us (61%)
  other arithmetic  178 us (15%)
  local copies, waits for them, and re-layouts  163 us (14%)
  matrix products  60.4 us (5%)
  starting transfers between devices  39 us (3%)
  between operations  16.7 us (1%)
    ppermute x6, waiting for transfers between devices, passed_along(): return lax.ppermute(x, axis, pairs)  397 us
    ppermute x3, waiting for transfers between devices, with_halo(): before = lax.ppermute(last, axis, up)  274 us
    scatter-add x3, other arithmetic, project_band(): spread = jnp.zeros((slab_rows.shape[0], panel_cols), jnp.float32).at[:, c...  133 us
    gather x3, local copies, waits for them, and re-layouts, spread_back(): picked = along_rows[:, columns]  83.9 us
    dynamic_update_slice x3, local copies, waits for them, and re-layouts, on_device(): lax.dynamic_update_slice_in_dim(jnp.zeros((3 * owner_rows, panel_cols), j...  46.3 us
    dot_general x3, matrix products, back_band(): jnp.dot(weights_band.T, window, precision=HIGH, preferred_element_type=jn...  39.2 us
    all_gather x3, waiting for transfers between devices, on_device(): wide_rows = lax.all_gather(residual, 'blk', axis=1, tiled=True)  29.2 us
  transfers between devices with their start and end apart: 18, of which 10 were waited for; matrix products, arithmetic and copies ran while one was open for 22% of the time, Pallas kernels for 0%

commit v1 on v0

v1 whole, which is shorter than its diff:
```python
import jax
import jax.numpy as jnp
from jax import lax
from jax.experimental import pallas as pl
from jax.experimental.pallas import tpu as pltpu
from jax.sharding import PartitionSpec as P

HIGH = lax.Precision.HIGHEST
F32 = jnp.float32
BF16 = jnp.bfloat16
LOW = 256
CHUNK = 1024
SLOT = 64


def split(x):
    high = x.astype(BF16)
    return high, (x - high.astype(F32)).astype(BF16)


def dot(a, b):
    return jnp.dot(a, b, preferred_element_type=F32)


def kernel(
    volume, col_index, col_weight, lanes, columns, measured, residual, gradient,
    low_hot, panel, frame, spread, from_core, mine, from_slabs, stack, wide, along,
    along_in, along_sum, along_core, taps_left, core_send, core_recv, slab_send, slab_recv,
    back_send, back_recv, last_send, last_recv, read_sem, write_sem,
):
    slab, blk = lax.axis_index("slab"), lax.axis_index("blk")
    slabs = lax.axis_size("slab")
    other = 1 - blk
    depth, cells = volume.shape
    views, rows, part = measured.shape
    groups = 2 * part // LOW
    chunks = cells // CHUNK
    has_lower, has_upper = slab > 0, slab < slabs - 1

    reads = [
        pltpu.make_async_copy(measured.at[v], frame.at[v], read_sem.at[v]) for v in range(views)
    ]
    for copy in reads:
        copy.start()
    barrier = pltpu.get_barrier_semaphore()
    pl.semaphore_signal(barrier, inc=1, device_id={"blk": other})

    @pl.when(has_lower)
    def _():
        pl.semaphore_signal(barrier, inc=1, device_id={"slab": slab - 1})

    @pl.when(has_upper)
    def _():
        pl.semaphore_signal(barrier, inc=1, device_id={"slab": slab + 1})

    pl.semaphore_wait(barrier, 1 + jnp.where(has_lower, 1, 0) + jnp.where(has_upper, 1, 0))

    def remote(source, target, send, recv, device):
        return pltpu.make_async_remote_copy(
            src_ref=source, dst_ref=target, send_sem=send, recv_sem=recv, device_id=device
        )

    def voxel_rows(v, j):
        at = pl.ds(pl.multiple_of(blk * cells + j * CHUNK, CHUNK), CHUNK)
        index, weight = col_index[v, :, at], col_weight[v, :, at]
        first, second = index[0:1], index[1:2]
        ordered = first <= second
        base = jnp.minimum(first, second)
        wa = jnp.where(ordered, weight[0:1], weight[1:2])
        wb = jnp.where(ordered, weight[1:2], weight[0:1])
        return lax.shift_right_logical(base, 8), lax.bitwise_and(base, LOW - 1), wa, wb

    my_cols = pl.ds(pl.multiple_of(blk * part, 128), part)
    other_cols = pl.ds(pl.multiple_of(other * part, 128), part)

    def core_copy(v):
        return remote(
            spread.at[v, :, other_cols], from_core.at[v], core_send.at[v], core_recv.at[v],
            {"blk": other},
        )

    def slab_copy(v, way):
        return remote(
            mine.at[v], from_slabs.at[v, 1 - way], slab_send.at[v, way],
            slab_recv.at[v, 1 - way], {"slab": slab + (2 * way - 1)},
        )

    def back_copy(v, way):
        return remote(
            along.at[v, pl.ds(2 * depth * way, depth)], along_in.at[v, 1 - way],
            back_send.at[v, way], back_recv.at[v, 1 - way], {"slab": slab + (2 * way - 1)},
        )

    def last_copy(v):
        return remote(
            along_sum.at[v], along_core.at[v], last_send.at[v], last_recv.at[v], {"blk": other}
        )

    def start_both(make, v):
        @pl.when(has_lower)
        def _():
            make(v, 0).start()

        @pl.when(has_upper)
        def _():
            make(v, 1).start()

    def await_both(make, v):
        @pl.when(has_lower)
        def _():
            make(v, 1).wait_recv()

        @pl.when(has_upper)
        def _():
            make(v, 0).wait_recv()

    def await_sent(make, v):
        @pl.when(has_lower)
        def _():
            make(v, 0).wait_send()

        @pl.when(has_upper)
        def _():
            make(v, 1).wait_send()

    @pl.when(slab == 0)
    def _():
        from_slabs[:, 0] = jnp.zeros((views, depth, part), F32)
        along_in[:, 0] = jnp.zeros((views, depth, part), F32)

    @pl.when(slab == slabs - 1)
    def _():
        from_slabs[:, 1] = jnp.zeros((views, depth, part), F32)
        along_in[:, 1] = jnp.zeros((views, depth, part), F32)

    def spread_view(v):
        panel[...] = jnp.zeros_like(panel)

        def step(j, carry):
            at = pl.ds(pl.multiple_of(j * CHUNK, CHUNK), CHUNK)
            high, low, wa, wb = voxel_rows(v, j)
            ids = lax.broadcasted_iota(jnp.int32, (LOW, CHUNK), 0)
            hot = jnp.where(ids == low, 1.0, 0.0).astype(BF16)
            low_hot[v, :, at] = hot
            values = volume[:, at]
            pieces = split(values * wa) + split(values * wb)
            high = jnp.broadcast_to(high, (depth, CHUNK))
            parts = []
            for h in range(groups):
                here = jnp.where(high == h, 1.0, 0.0).astype(BF16)
                parts += [piece * here for piece in pieces]
            panel[...] += lax.dot_general(
                jnp.concatenate(parts, axis=0), hot, (((1,), (1,)), ((), ())),
                preferred_element_type=F32,
            )
            return carry

        lax.fori_loop(0, chunks, step, 0)
        for h in range(groups):
            own = panel[4 * depth * h : 4 * depth * (h + 1)]
            at = slice(LOW * h, LOW * (h + 1))
            spread[v, :, at] = own[0:depth] + own[depth : 2 * depth]
            wide[:, at] = own[2 * depth : 3 * depth] + own[3 * depth :]
        spread[v] = spread[v] + pltpu.roll(wide[...], 1, 1)

    def pass_on(v):
        core_copy(v).wait_recv()
        mine[v] = spread[v, :, my_cols] + from_core[v]
        start_both(slab_copy, v)

    for v in range(views):
        spread_view(v)
        core_copy(v).start()
        if v > 0:
            pass_on(v - 1)

    def row_matrices(v):
        ids = lax.broadcasted_iota(jnp.int32, (rows, 4 * SLOT), 0).astype(F32)
        p = lanes[v]
        project = jnp.where(ids == p[0:1], p[2:3], 0.0) + jnp.where(ids == p[1:2], p[3:4], 0.0)
        ids = lax.broadcasted_iota(jnp.int32, (SLOT, rows), 1).astype(F32)
        p = columns[v]
        back = jnp.where(ids == p[:, 0:1], p[:, 4:5], 0.0)
        back = back + jnp.where(ids == p[:, 1:2], p[:, 5:6], 0.0)
        return project, back

    def by_slot(x):
        high, low = split(x)
        slot = lax.broadcasted_iota(jnp.int32, x.shape, 1) < 2 * SLOT
        return jnp.where(slot, high.astype(F32), low.astype(F32)).astype(BF16)

    mixes, projects = [], []
    for v in range(views):
        if v == 1:
            pass_on(views - 1)
        project, back = row_matrices(v)
        mixes.append(
            by_slot(jnp.dot(back, project, precision=HIGH, preferred_element_type=F32))
        )
        projects.append(by_slot(project))
        back_high, back_low = split(back)
        reads[v].wait()
        data_high, data_low = split(frame[v])
        both = dot(jnp.concatenate([back_high, back_low], axis=0), data_high)
        along[v] = both[:SLOT] + both[SLOT:] + dot(back_high, data_low)

    for v in range(views):
        await_both(slab_copy, v)
        slices = jnp.concatenate(
            [from_slabs[v, 0], mine[v], from_slabs[v, 1], jnp.zeros((SLOT - 3 * depth, part), F32)],
            axis=0,
        )
        high, low = split(slices)
        stack[v, 0:SLOT] = high
        stack[v, SLOT : 2 * SLOT] = low
        stack[v, 2 * SLOT : 3 * SLOT] = high
        stack[v, 3 * SLOT :] = low
        along[v] = along[v] - dot(mixes[v], stack[v])
        start_both(back_copy, v)

    writes = [
        pltpu.make_async_copy(frame.at[v], residual.at[v], write_sem.at[v]) for v in range(views)
    ]

    def collect(v):
        await_both(back_copy, v)
        along_sum[v] = along[v, depth : 2 * depth] + along_in[v, 0] + along_in[v, 1]
        last_copy(v).start()

    for v in range(views):
        frame[v] = frame[v] - dot(projects[v], stack[v])
        writes[v].start()
        collect(v)

    gradient[...] = jnp.zeros_like(gradient)
    for v in range(views):
        last_copy(v).wait_recv()
        wide[:, my_cols] = along_sum[v]
        wide[:, other_cols] = along_core[v]
        here = wide[...]
        for t, values in enumerate((here, pltpu.roll(here, 2 * part - 1, 1))):
            for piece, x in enumerate(split(values)):
                for h in range(groups):
                    taps_left[piece, t, depth * h : depth * (h + 1)] = x[:, LOW * h : LOW * (h + 1)]

        def step(j, carry):
            at = pl.ds(pl.multiple_of(j * CHUNK, CHUNK), CHUNK)
            high, _, wa, wb = voxel_rows(v, j)
            high = jnp.broadcast_to(high, (depth, CHUNK))
            hot = low_hot[v, :, at]
            total = gradient[:, at]
            for t, w in enumerate((wa, wb)):
                picked = dot(taps_left[0, t], hot) + dot(taps_left[1, t], hot)
                found = picked[:depth]
                for h in range(1, groups):
                    found = jnp.where(high == h, picked[depth * h : depth * (h + 1)], found)
                total = total + found * w
            gradient[:, at] = total
            return carry

        lax.fori_loop(0, chunks, step, 0)
    gradient[...] = gradient[...] * (1.0 / views)

    for v in range(views):
        core_copy(v).wait_send()
        await_sent(slab_copy, v)
        await_sent(back_copy, v)
        last_copy(v).wait_send()
        writes[v].wait()


def on_device(
    volume, measured, band_start, band_length, row_offset, row_weight, col_index, col_weight
):
    slab = lax.axis_index("slab")
    depth, cells = volume.shape
    views, rows, part = measured.shape
    taps = row_offset.shape[1]
    start = jnp.repeat(band_start, depth, axis=1)[:, None, :]
    length = jnp.repeat(band_length, depth, axis=1)[:, None, :]
    row = (start + row_offset - slab * rows).astype(F32)
    live = jnp.where(row_offset < length, row_weight, 0.0)
    rest = jnp.zeros((views, 8 - 3 * taps, row.shape[2]), F32)
    table = jnp.concatenate([row, row_weight, live, rest], axis=1)
    table = jnp.pad(table, ((0, 0), (0, 0), (depth, depth)))
    table = lax.dynamic_slice_in_dim(table, slab * depth, 3 * depth, 2)
    table = jnp.pad(table, ((0, 0), (0, 0), (0, SLOT - 3 * depth)))
    lanes = jnp.tile(table, (1, 1, 4))
    columns = jnp.swapaxes(table, 1, 2)

    vmem, dma = pltpu.VMEM, pltpu.SemaphoreType.DMA
    in_vmem, anywhere = pl.BlockSpec(memory_space=pltpu.VMEM), pl.BlockSpec(memory_space=pl.ANY)
    groups = 2 * part // LOW
    return pl.pallas_call(
        kernel,
        out_shape=(
            jax.ShapeDtypeStruct(measured.shape, F32),
            jax.ShapeDtypeStruct(volume.shape, F32),
        ),
        in_specs=[in_vmem] * 5 + [anywhere],
        out_specs=(anywhere, in_vmem),
        scratch_shapes=[
            vmem((views, LOW, cells), BF16),
            vmem((4 * depth * groups, LOW), F32),
            vmem((views, rows, part), F32),
            vmem((views, depth, 2 * part), F32),
            vmem((views, depth, part), F32),
            vmem((views, depth, part), F32),
            vmem((views, 2, depth, part), F32),
            vmem((views, 4 * SLOT, part), BF16),
            vmem((depth, 2 * part), F32),
            vmem((views, SLOT, part), F32),
            vmem((views, 2, depth, part), F32),
            vmem((views, depth, part), F32),
            vmem((views, depth, part), F32),
            vmem((2, 2, depth * groups, LOW), BF16),
            dma((views,)),
            dma((views,)),
            dma((views, 2)),
            dma((views, 2)),
            dma((views, 2)),
            dma((views, 2)),
            dma((views,)),
            dma((views,)),
            dma((views,)),
            dma((views,)),
        ],
        compiler_params=pltpu.CompilerParams(
            collective_id=0, has_side_effects=True, vmem_limit_bytes=56 * 1024 * 1024
        ),
    )(volume, col_index, col_weight, lanes, columns, measured)


def solution(mesh):
    return jax.shard_map(
        on_device,
        mesh=mesh,
        in_specs=(P(("grp", "slab"), "blk"), P("grp", "slab", "blk"), P(), P(), P(), P(), P(), P()),
        out_specs=(P("grp", "slab", "blk"), P(("grp", "slab"), "blk")),
        check_vma=False,
    )
```

time: 1180 us -> 56.9 us (0.05)
  the two profiles are of different devices: /device:TPU:0 before, /device:TPU:15 now
where the time goes in v1:
time: 56.9 us; the launch traced here: 56.6 us
  Pallas kernels  45 us (79%)
  local copies, waits for them, and re-layouts  8.86 us (16%)
  other arithmetic  2.1 us (4%)
  between operations  0.68 us (1%)
    pallas_call x1, Pallas kernels, on_device(): pl.pallas_call(kernel, out_shape=(jax.ShapeDtypeStruct(measured.shape, F3...  45 us
    unnamed x5, local copies, waits for them, and re-layouts  5.66 us

profile of v1, /device:TPU:15, one launch (start us, length us, event | category | flops | bytes accessed | tf_op | source)
XLA Modules:
  0.0 56.6 jit_solution(15651490221142137272)
XLA Ops:
  0.6 0.8 %broadcast_in_dim.11 = s32[3,8,16]{2,1,0:T(8,128)S(1)} broadcast(s32[3,8]{1,0:T(4,128)} %param.10), dimensions={0,1} | broadcast | bytes 1632 | tf_op jit(solution)/shard_map/broadcast_in_dim | solution.py:279
  1.4 0.1 add.17
  1.5 0.7 %subtract_convert_fusion = f32[3,2,128]{2,1,0:T(2,128)S(1)} fusion(s32[3,2,128]{2,1,0:T(2,128)} %param.12, s32[]{:T(128)S(6)} %mul.6, s32[3,128]{1,0:T(4,128)S(1)} %add.17), kind=kLoop, calls=%fused_computation.4 | loop fusion | flops 2304 | bytes 7684 | tf_op jit(solution)/shard_map/convert_element_type | solution.py:281
  2.2 0.8 %broadcast_in_dim.12 = s32[3,8,16]{2,1,0:T(8,128)S(1)} broadcast(s32[3,8]{1,0:T(4,128)} %param.11), dimensions={0,1} | broadcast | bytes 1632 | tf_op jit(solution)/shard_map/broadcast_in_dim | solution.py:280
  2.9 0.1 lt.13
  3.0 0.7 %compare_select_fusion = f32[3,2,128]{2,1,0:T(2,128)S(1)} fusion(f32[3,2,128]{2,1,0:T(2,128)} %param.13, s32[3,2,128]{2,1,0:T(2,128)} %param.12, s32[3,128]{1,0:T(4,128)S(1)} %lt.13), kind=kLoop, calls=%fused_computation.3 | loop fusion | flops 1536 | bytes 10752 | tf_op jit(solution)/shard_map/jit(_where)/select_n | solution.py:282
  3.7 0.7 %pad_maximum_fusion = f32[3,8,128]{2,1,0:T(8,128)S(1)} fusion(f32[3,2,128]{2,1,0:T(2,128)S(1)} %broadcast_in_dim.13, f32[3,2,128]{2,1,0:T(2,128)S(1)} %compare_select_fusion, f32[3,2,128]{2,1,0:T(2,128)} %param.13, f32[3,2,128]{2,1,0:T(2,128)S(1)} %subtract_convert_fusion), kind=kLoop, calls=%fused_computation.1 | loop fusion | flops 9216 | bytes 24576 | tf_op jit(solution)/shard_map/concatenate | solution.py:284
  4.4 0.1 copy.18
  4.6 0.1 copy.20
  4.6 0.7 %pad_bitcast_fusion.columns = f32[3,64,8]{2,1,0:T(8,128)} fusion(f32[3,8,48]{1,2,0:T(8,128)S(1)} %pad_dynamic-slice_fusion), kind=kLoop, calls=%fused_computation.2 | loop fusion | bytes 10752 | tf_op jit(solution)/shard_map/transpose | solution.py:289
  5.3 0.7 %tile.10.lanes = f32[3,8,256]{2,1,0:T(8,128)} reshape(f32[3,8,4,64]{3,2,1,0:T(4,128)S(1)} %tile.4) | data formatting | bytes 49152 | tf_op jit(solution)/shard_map/tile | solution.py:288
  6.0 45.0 %shard_map.95 = (f32[3,256,1536]{2,1,0:T(8,128)}, f32[16,4096]{1,0:T(8,128)}) custom-call(f32[16,4096]{1,0:T(8,128)} %volume.1, s32[3,2,8192]{2,1,0:T(2,128)} %col_index.1, f32[3,2,8192]{2,1,0:T(2,128)} %col_weight.1, f32[3,8,256]{2,1,0:T(8,128)} %tile.10.lanes, f32[3,64,8]{2,1,0:T(8,128)} %pad_bitcast_fusion.columns, f32[3,256,1536]{2,1,0:T(8,128)} %measured.1), custom_call_target="tpu_custom_call" | custom-call | tf_op jit(solution)/shard_map/pallas_call | solution.py:294
  51.0 0.0 copy-start
  51.0 4.9 %copy.23 = f32[3,256,1536]{2,1,0:T(8,128)} copy(f32[3,256,1536]{2,1,0:T(8,128)} %get-tuple-element.4) | data formatting | bytes 9437184
  55.9 0.0 copy-done
  55.9 0.7 %copy.24 = f32[16,4096]{1,0:T(8,128)} copy(f32[16,4096]{1,0:T(8,128)S(1)} %copy-done) | data formatting | bytes 524288
  (4 shorter events, 0.0 us)
Async XLA Ops:
  51.0 4.9 %copy-start = (f32[16,4096]{1,0:T(8,128)S(1)}, f32[16,4096]{1,0:T(8,128)}, u32[]{:S(2)}) copy-start(f32[16,4096]{1,0:T(8,128)} %get-tuple-element.5) | copy-start | bytes 786436

commit v2 on v1

--- a/solution.py
+++ b/solution.py
@@ -22,11 +22,17 @@
     return jnp.dot(a, b, preferred_element_type=F32)
 
 
+def order_of(views):
+    turns = [(step + 2 * view, -view, step, view) for view in range(views) for step in range(9)]
+    return [(step, view) for _, _, step, view in sorted(turns)]
+
+
 def kernel(
     volume, col_index, col_weight, lanes, columns, measured, residual, gradient,
-    low_hot, panel, frame, spread, from_core, mine, from_slabs, stack, wide, along,
-    along_in, along_sum, along_core, taps_left, core_send, core_recv, slab_send, slab_recv,
-    back_send, back_recv, last_send, last_recv, read_sem, write_sem,
+    low_hot, panel, frame, spread, from_core, mine, from_pair, from_far, stack, wide, along,
+    far_in, pair_out, pair_in, along_sum, along_core, taps_left, core_send, core_recv,
+    pair_send, pair_recv, pass_send, pass_recv, far_send, far_recv, near_send, near_recv,
+    last_send, last_recv, read_sem, write_sem,
 ):
     slab, blk = lax.axis_index("slab"), lax.axis_index("blk")
     slabs = lax.axis_size("slab")
@@ -35,7 +41,10 @@
     views, rows, part = measured.shape
     groups = 2 * part // LOW
     chunks = cells // CHUNK
-    has_lower, has_upper = slab > 0, slab < slabs - 1
+    pair = slab + 1 - 2 * lax.rem(slab, 2)
+    onward, backward = slab + 2 * (pair - slab), slab - 2 * (pair - slab)
+    has_onward = jnp.logical_and(onward >= 0, onward < slabs)
+    has_backward = jnp.logical_and(backward >= 0, backward < slabs)
 
     reads = [
         pltpu.make_async_copy(measured.at[v], frame.at[v], read_sem.at[v]) for v in range(views)
@@ -45,15 +54,17 @@
     barrier = pltpu.get_barrier_semaphore()
     pl.semaphore_signal(barrier, inc=1, device_id={"blk": other})
 
-    @pl.when(has_lower)
+    pl.semaphore_signal(barrier, inc=1, device_id={"slab": pair})
+
+    @pl.when(has_onward)
     def _():
-        pl.semaphore_signal(barrier, inc=1, device_id={"slab": slab - 1})
-
-    @pl.when(has_upper)
+        pl.semaphore_signal(barrier, inc=1, device_id={"slab": onward})
+
+    @pl.when(has_backward)
     def _():
-        pl.semaphore_signal(barrier, inc=1, device_id={"slab": slab + 1})
-
-    pl.semaphore_wait(barrier, 1 + jnp.where(has_lower, 1, 0) + jnp.where(has_upper, 1, 0))
+        pl.semaphore_signal(barrier, inc=1, device_id={"slab": backward})
+
+    pl.semaphore_wait(barrier, 2 + jnp.where(has_onward, 1, 0) + jnp.where(has_backward, 1, 0))
 
     def remote(source, target, send, recv, device):
         return pltpu.make_async_remote_copy(
@@ -79,16 +90,25 @@
             {"blk": other},
         )
 
-    def slab_copy(v, way):
-        return remote(
-            mine.at[v], from_slabs.at[v, 1 - way], slab_send.at[v, way],
-            slab_recv.at[v, 1 - way], {"slab": slab + (2 * way - 1)},
-        )
-
-    def back_copy(v, way):
-        return remote(
-            along.at[v, pl.ds(2 * depth * way, depth)], along_in.at[v, 1 - way],
-            back_send.at[v, way], back_recv.at[v, 1 - way], {"slab": slab + (2 * way - 1)},
+    def pair_copy(v):
+        return remote(
+            mine.at[v], from_pair.at[v], pair_send.at[v], pair_recv.at[v], {"slab": pair}
+        )
+
+    def pass_copy(v):
+        return remote(
+            from_pair.at[v], from_far.at[v], pass_send.at[v], pass_recv.at[v], {"slab": onward}
+        )
+
+    def far_copy(v):
+        return remote(
+            along.at[v, pl.ds(2 * depth, depth)], far_in.at[v], far_send.at[v], far_recv.at[v],
+            {"slab": backward},
+        )
+
+    def near_copy(v):
+        return remote(
+            pair_out.at[v], pair_in.at[v], near_send.at[v], near_recv.at[v], {"slab": pair}
         )
 
     def last_copy(v):
@@ -96,42 +116,13 @@
             along_sum.at[v], along_core.at[v], last_send.at[v], last_recv.at[v], {"blk": other}
         )
 
-    def start_both(make, v):
-        @pl.when(has_lower)
-        def _():
-            make(v, 0).start()
-
-        @pl.when(has_upper)
-        def _():
-            make(v, 1).start()
-
-    def await_both(make, v):
-        @pl.when(has_lower)
-        def _():
-            make(v, 1).wait_recv()
-
-        @pl.when(has_upper)
-        def _():
-            make(v, 0).wait_recv()
-
-    def await_sent(make, v):
-        @pl.when(has_lower)
-        def _():
-            make(v, 0).wait_send()
-
-        @pl.when(has_upper)
-        def _():
-            make(v, 1).wait_send()
-
-    @pl.when(slab == 0)
+    @pl.when(jnp.logical_not(has_backward))
     def _():
-        from_slabs[:, 0] = jnp.zeros((views, depth, part), F32)
-        along_in[:, 0] = jnp.zeros((views, depth, part), F32)
-
-    @pl.when(slab == slabs - 1)
+        from_far[...] = jnp.zeros_like(from_far)
+
+    @pl.when(jnp.logical_not(has_onward))
     def _():
-        from_slabs[:, 1] = jnp.zeros((views, depth, part), F32)
-        along_in[:, 1] = jnp.zeros((views, depth, part), F32)
+        far_in[...] = jnp.zeros_like(far_in)
 
     def spread_view(v):
         panel[...] = jnp.zeros_like(panel)
@@ -163,17 +154,6 @@
             wide[:, at] = own[2 * depth : 3 * depth] + own[3 * depth :]
         spread[v] = spread[v] + pltpu.roll(wide[...], 1, 1)
 
-    def pass_on(v):
-        core_copy(v).wait_recv()
-        mine[v] = spread[v, :, my_cols] + from_core[v]
-        start_both(slab_copy, v)
-
-    for v in range(views):
-        spread_view(v)
-        core_copy(v).start()
-        if v > 0:
-            pass_on(v - 1)
-
     def row_matrices(v):
         ids = lax.broadcasted_iota(jnp.int32, (rows, 4 * SLOT), 0).astype(F32)
         p = lanes[v]
@@ -189,51 +169,69 @@
         slot = lax.broadcasted_iota(jnp.int32, x.shape, 1) < 2 * SLOT
         return jnp.where(slot, high.astype(F32), low.astype(F32)).astype(BF16)
 
-    mixes, projects = [], []
-    for v in range(views):
-        if v == 1:
-            pass_on(views - 1)
+    def measured_along(v):
         project, back = row_matrices(v)
-        mixes.append(
-            by_slot(jnp.dot(back, project, precision=HIGH, preferred_element_type=F32))
-        )
-        projects.append(by_slot(project))
+        mix = by_slot(jnp.dot(back, project, precision=HIGH, preferred_element_type=F32))
         back_high, back_low = split(back)
         reads[v].wait()
         data_high, data_low = split(frame[v])
         both = dot(jnp.concatenate([back_high, back_low], axis=0), data_high)
         along[v] = both[:SLOT] + both[SLOT:] + dot(back_high, data_low)
-
-    for v in range(views):
-        await_both(slab_copy, v)
+        return mix, by_slot(project)
+
+    writes = [
+        pltpu.make_async_copy(frame.at[v], residual.at[v], write_sem.at[v]) for v in range(views)
+    ]
+
+    def subtract(v, project):
+        frame[v] = frame[v] - dot(project, stack[v])
+        writes[v].start()
+
+    def to_pair(v):
+        core_copy(v).wait_recv()
+        mine[v] = spread[v, :, my_cols] + from_core[v]
+        pair_copy(v).start()
+
+    def to_onward(v):
+        pair_copy(v).wait_recv()
+
+        @pl.when(has_onward)
+        def _():
+            pass_copy(v).start()
+
+    def to_backward(v, mix):
+        @pl.when(has_backward)
+        def _():
+            pass_copy(v).wait_recv()
+
         slices = jnp.concatenate(
-            [from_slabs[v, 0], mine[v], from_slabs[v, 1], jnp.zeros((SLOT - 3 * depth, part), F32)],
-            axis=0,
+            [from_pair[v], mine[v], from_far[v], jnp.zeros((SLOT - 3 * depth, part), F32)], axis=0
         )
         high, low = split(slices)
         stack[v, 0:SLOT] = high
         stack[v, SLOT : 2 * SLOT] = low
         stack[v, 2 * SLOT : 3 * SLOT] = high
         stack[v, 3 * SLOT :] = low
-        along[v] = along[v] - dot(mixes[v], stack[v])
-        start_both(back_copy, v)
-
-    writes = [
-        pltpu.make_async_copy(frame.at[v], residual.at[v], write_sem.at[v]) for v in range(views)
-    ]
-
-    def collect(v):
-        await_both(back_copy, v)
-        along_sum[v] = along[v, depth : 2 * depth] + along_in[v, 0] + along_in[v, 1]
+        along[v] = along[v] - dot(mix, stack[v])
+
+        @pl.when(has_backward)
+        def _():
+            far_copy(v).start()
+
+    def along_to_pair(v):
+        @pl.when(has_onward)
+        def _():
+            far_copy(v).wait_recv()
+
+        pair_out[v] = along[v, 0:depth] + far_in[v]
+        near_copy(v).start()
+
+    def along_to_core(v):
+        near_copy(v).wait_recv()
+        along_sum[v] = along[v, depth : 2 * depth] + pair_in[v]
         last_copy(v).start()
 
-    for v in range(views):
-        frame[v] = frame[v] - dot(projects[v], stack[v])
-        writes[v].start()
-        collect(v)
-
-    gradient[...] = jnp.zeros_like(gradient)
-    for v in range(views):
+    def gather_view(v):
         last_copy(v).wait_recv()
         wide[:, my_cols] = along_sum[v]
         wide[:, other_cols] = along_core[v]
@@ -248,24 +246,54 @@
             high, _, wa, wb = voxel_rows(v, j)
             high = jnp.broadcast_to(high, (depth, CHUNK))
             hot = low_hot[v, :, at]
-            total = gradient[:, at]
+            total = jnp.zeros((depth, CHUNK), F32) if v == 0 else gradient[:, at]
             for t, w in enumerate((wa, wb)):
                 picked = dot(taps_left[0, t], hot) + dot(taps_left[1, t], hot)
                 found = picked[:depth]
                 for h in range(1, groups):
                     found = jnp.where(high == h, picked[depth * h : depth * (h + 1)], found)
                 total = total + found * w
-            gradient[:, at] = total
+            gradient[:, at] = total * (1.0 / views) if v == views - 1 else total
             return carry
 
         lax.fori_loop(0, chunks, step, 0)
-    gradient[...] = gradient[...] * (1.0 / views)
+    mixes, projects = {}, {}
+
+    def prepare(v):
+        mixes[v], projects[v] = measured_along(v)
+
+    def begin(v):
+        spread_view(v)
+        core_copy(v).start()
+
+    steps = (
+        begin,
+        to_pair,
+        prepare,
+        to_onward,
+        lambda v: to_backward(v, mixes[v]),
+        along_to_pair,
+        lambda v: subtract(v, projects[v]),
+        along_to_core,
+        gather_view,
+    )
+    for turn in order_of(views):
+        steps[turn[0]](turn[1])
 
     for v in range(views):
         core_copy(v).wait_send()
-        await_sent(slab_copy, v)
-        await_sent(back_copy, v)
+        pair_copy(v).wait_send()
+        near_copy(v).wait_send()
         last_copy(v).wait_send()
+
+        @pl.when(has_onward)
+        def _():
+            pass_copy(v).wait_send()
+
+        @pl.when(has_backward)
+        def _():
+            far_copy(v).wait_send()
+
         writes[v].wait()
 
 
@@ -283,7 +311,14 @@
     rest = jnp.zeros((views, 8 - 3 * taps, row.shape[2]), F32)
     table = jnp.concatenate([row, row_weight, live, rest], axis=1)
     table = jnp.pad(table, ((0, 0), (0, 0), (depth, depth)))
-    table = lax.dynamic_slice_in_dim(table, slab * depth, 3 * depth, 2)
+    pair = slab + 1 - 2 * lax.rem(slab, 2)
+    table = jnp.concatenate(
+        [
+            lax.dynamic_slice_in_dim(table, (at + 1) * depth, depth, 2)
+            for at in (pair, slab, 2 * slab - pair)
+        ],
+        axis=2,
+    )
     table = jnp.pad(table, ((0, 0), (0, 0), (0, SLOT - 3 * depth)))
     lanes = jnp.tile(table, (1, 1, 4))
     columns = jnp.swapaxes(table, 1, 2)
@@ -306,25 +341,19 @@
             vmem((views, depth, 2 * part), F32),
             vmem((views, depth, part), F32),
             vmem((views, depth, part), F32),
-            vmem((views, 2, depth, part), F32),
+            vmem((views, depth, part), F32),
+            vmem((views, depth, part), F32),
             vmem((views, 4 * SLOT, part), BF16),
             vmem((depth, 2 * part), F32),
             vmem((views, SLOT, part), F32),
-            vmem((views, 2, depth, part), F32),
+            vmem((views, depth, part), F32),
+            vmem((views, depth, part), F32),
+            vmem((views, depth, part), F32),
             vmem((views, depth, part), F32),
             vmem((views, depth, part), F32),
             vmem((2, 2, depth * groups, LOW), BF16),
-            dma((views,)),
-            dma((views,)),
-            dma((views, 2)),
-            dma((views, 2)),
-            dma((views, 2)),
-            dma((views, 2)),
-            dma((views,)),
-            dma((views,)),
-            dma((views,)),
-            dma((views,)),
-        ],
+        ]
+        + [dma((views,))] * 14,
         compiler_params=pltpu.CompilerParams(
             collective_id=0, has_side_effects=True, vmem_limit_bytes=56 * 1024 * 1024
         ),

time: 56.9 us -> 51.1 us (0.90)
  the two profiles are of different devices: /device:TPU:15 before, /device:TPU:0 now
where the time goes in v2:
time: 51.1 us; the launch traced here: 50.7 us
  Pallas kernels  38.9 us (76%)
  local copies, waits for them, and re-layouts  8.9 us (17%)
  other arithmetic  2.26 us (4%)
  between operations  0.69 us (1%)
    pallas_call x1, Pallas kernels, on_device(): pl.pallas_call(kernel, out_shape=(jax.ShapeDtypeStruct(measured.shape, F3...  38.9 us
    unnamed x5, local copies, waits for them, and re-layouts  5.66 us

profile of v2, /device:TPU:0, one launch (start us, length us, event | category | flops | bytes accessed | tf_op | source)
XLA Modules:
  0.0 50.7 jit_solution(14475011275200265007)
XLA Ops:
  0.7 0.8 %broadcast_in_dim.11 = s32[3,8,16]{2,1,0:T(8,128)S(1)} broadcast(s32[3,8]{1,0:T(4,128)} %param.10), dimensions={0,1} | broadcast | bytes 1632 | tf_op jit(solution)/shard_map/broadcast_in_dim | solution.py:307
  1.4 0.1 add.33
  1.5 0.7 %subtract_convert_fusion = f32[3,2,128]{2,1,0:T(2,128)S(1)} fusion(s32[3,2,128]{2,1,0:T(2,128)} %param.12, s32[]{:T(128)S(6)} %mul.18, s32[3,128]{1,0:T(4,128)S(1)} %add.33), kind=kLoop, calls=%fused_computation.9 | loop fusion | flops 2304 | bytes 7684 | tf_op jit(solution)/shard_map/convert_element_type | solution.py:309
  2.2 0.8 %broadcast_in_dim.12 = s32[3,8,16]{2,1,0:T(8,128)S(1)} broadcast(s32[3,8]{1,0:T(4,128)} %param.11), dimensions={0,1} | broadcast | bytes 1632 | tf_op jit(solution)/shard_map/broadcast_in_dim | solution.py:308
  2.9 0.1 lt.19
  3.0 0.7 %compare_select_fusion = f32[3,2,128]{2,1,0:T(2,128)S(1)} fusion(f32[3,2,128]{2,1,0:T(2,128)} %param.13, s32[3,2,128]{2,1,0:T(2,128)} %param.12, s32[3,128]{1,0:T(4,128)S(1)} %lt.19), kind=kLoop, calls=%fused_computation.8 | loop fusion | flops 1536 | bytes 10752 | tf_op jit(solution)/shard_map/jit(_where)/select_n | solution.py:310
  3.7 0.8 %select_maximum_fusion = f32[3,8,160]{2,1,0:T(8,128)S(1)} fusion(f32[3,2,128]{2,1,0:T(2,128)S(1)} %broadcast_in_dim.13, f32[3,2,128]{2,1,0:T(2,128)S(1)} %compare_select_fusion, f32[3,2,128]{2,1,0:T(2,128)} %param.13, f32[3,2,128]{2,1,0:T(2,128)S(1)} %subtract_convert_fusion), kind=kLoop, calls=%fused_computation.2 | loop fusion | flops 38400 | bytes 27648 | tf_op jit(solution)/shard_map/concatenate | solution.py:312
  4.5 0.1 constant_dynamic-slice_fusion.2
  4.6 0.1 pad_maximum_fusion
  4.7 0.1 copy.18
  4.8 0.1 copy.20
  4.8 0.7 %pad_bitcast_fusion.columns = f32[3,64,8]{2,1,0:T(8,128)} fusion(f32[3,8,48]{1,2,0:T(8,128)S(1)} %copy.18), kind=kLoop, calls=%fused_computation.7 | loop fusion | bytes 10752 | tf_op jit(solution)/shard_map/transpose | solution.py:324
  5.5 0.7 %tile.10.lanes = f32[3,8,256]{2,1,0:T(8,128)} reshape(f32[3,8,4,64]{3,2,1,0:T(4,128)S(1)} %tile.4) | data formatting | bytes 49152 | tf_op jit(solution)/shard_map/tile | solution.py:323
  6.2 38.9 %shard_map.95 = (f32[3,256,1536]{2,1,0:T(8,128)}, f32[16,4096]{1,0:T(8,128)}) custom-call(f32[16,4096]{1,0:T(8,128)} %volume.1, s32[3,2,8192]{2,1,0:T(2,128)} %col_index.1, f32[3,2,8192]{2,1,0:T(2,128)} %col_weight.1, f32[3,8,256]{2,1,0:T(8,128)} %tile.10.lanes, f32[3,64,8]{2,1,0:T(8,128)} %pad_bitcast_fusion.columns, f32[3,256,1536]{2,1,0:T(8,128)} %measured.1), custom_call_target="tpu_custom_call" | custom-call | tf_op jit(solution)/shard_map/pallas_call | solution.py:329
  45.1 0.0 copy-start
  45.2 4.9 %copy.23 = f32[3,256,1536]{2,1,0:T(8,128)} copy(f32[3,256,1536]{2,1,0:T(8,128)} %get-tuple-element.7) | data formatting | bytes 9437184
  50.0 0.0 copy-done
  50.0 0.7 %copy.24 = f32[16,4096]{1,0:T(8,128)} copy(f32[16,4096]{1,0:T(8,128)S(1)} %copy-done) | data formatting | bytes 524288
  (3 shorter events, 0.0 us)
Async XLA Ops:
  45.1 4.9 %copy-start = (f32[16,4096]{1,0:T(8,128)S(1)}, f32[16,4096]{1,0:T(8,128)}, u32[]{:S(2)}) copy-start(f32[16,4096]{1,0:T(8,128)} %get-tuple-element.8) | copy-start | bytes 786436

commit v3 on v2

--- a/solution.py
+++ b/solution.py
@@ -22,13 +22,17 @@
     return jnp.dot(a, b, preferred_element_type=F32)
 
 
-def order_of(views):
-    turns = [(step + 2 * view, -view, step, view) for view in range(views) for step in range(9)]
-    return [(step, view) for _, _, step, view in sorted(turns)]
+ORDER = (
+    ("b", 0), ("b", 1), ("p", 0), ("b", 2), ("p", 1), ("t", 0), ("o", 0), ("t", 1), ("p", 2),
+    ("m", 0), ("o", 1), ("w", 0), ("t", 2), ("m", 1), ("o", 2), ("w", 1), ("a", 0), ("m", 2),
+    ("w", 2), ("a", 1), ("s", 0), ("s", 1), ("c", 0), ("a", 2), ("s", 2), ("c", 1), ("g", 0),
+    ("c", 2), ("g", 1), ("g", 2),
+)
 
 
 def kernel(
-    volume, col_index, col_weight, lanes, columns, measured, residual, gradient,
+    volume, col_index, col_weight, row_offset, row_weight, band_start, band_length, measured,
+    residual, gradient,
     low_hot, panel, frame, spread, from_core, mine, from_pair, from_far, stack, wide, along,
     far_in, pair_out, pair_in, along_sum, along_core, taps_left, core_send, core_recv,
     pair_send, pair_recv, pass_send, pass_recv, far_send, far_recv, near_send, near_recv,
@@ -64,7 +68,8 @@
     def _():
         pl.semaphore_signal(barrier, inc=1, device_id={"slab": backward})
 
-    pl.semaphore_wait(barrier, 2 + jnp.where(has_onward, 1, 0) + jnp.where(has_backward, 1, 0))
+    def await_barrier():
+        pl.semaphore_wait(barrier, 2 + jnp.where(has_onward, 1, 0) + jnp.where(has_backward, 1, 0))
 
     def remote(source, target, send, recv, device):
         return pltpu.make_async_remote_copy(
@@ -154,12 +159,36 @@
             wide[:, at] = own[2 * depth : 3 * depth] + own[3 * depth :]
         spread[v] = spread[v] + pltpu.roll(wide[...], 1, 1)
 
+    def row_table(v):
+        slices = row_offset.shape[2]
+        raw = jnp.concatenate(
+            [row_offset[v].astype(F32), row_weight[v], jnp.zeros((4, slices), F32)], axis=0
+        )
+        lane = lax.broadcasted_iota(jnp.int32, (8, 4 * SLOT // 2), 1)
+        table = jnp.zeros((8, 4 * SLOT // 2), F32)
+        start, length = jnp.zeros_like(table), jnp.zeros_like(table)
+        for place, at in enumerate((pair, slab, 2 * slab - pair)):
+            shift = lax.rem((place - at) * depth + 2 * slices, slices)
+            here = jnp.logical_and(lane >= place * depth, lane < (place + 1) * depth)
+            table = jnp.where(here, pltpu.roll(raw, shift, 1)[:, : 2 * SLOT], table)
+            held = jnp.clip(at, 0, slabs - 1)
+            start = jnp.where(here, (band_start[v, held] - slab * rows).astype(F32), start)
+            length = jnp.where(here, band_length[v, held].astype(F32), length)
+        last = jnp.where(has_backward, 3 * depth, 2 * depth)
+        table = jnp.where(lane < last, table, 0.0)
+        offset, weight = table[0:2], table[2:4]
+        live = jnp.where(offset < length[0:2], weight, 0.0)
+        row = jnp.where(lane[0:2] < last, offset + start[0:2], 0.0)
+        return jnp.concatenate([row, weight, live, jnp.zeros((2, 2 * SLOT), F32)], axis=0)
+
     def row_matrices(v):
+        table = row_table(v)
+        p = table + pltpu.roll(table, SLOT, 1)
+        p = jnp.concatenate([p, p], axis=1)
         ids = lax.broadcasted_iota(jnp.int32, (rows, 4 * SLOT), 0).astype(F32)
-        p = lanes[v]
         project = jnp.where(ids == p[0:1], p[2:3], 0.0) + jnp.where(ids == p[1:2], p[3:4], 0.0)
+        p = jnp.concatenate([table, jnp.zeros((2 * SLOT - 8, 2 * SLOT), F32)], axis=0).T[:SLOT]
         ids = lax.broadcasted_iota(jnp.int32, (SLOT, rows), 1).astype(F32)
-        p = columns[v]
         back = jnp.where(ids == p[:, 0:1], p[:, 4:5], 0.0)
         back = back + jnp.where(ids == p[:, 1:2], p[:, 5:6], 0.0)
         return project, back
@@ -169,22 +198,26 @@
         slot = lax.broadcasted_iota(jnp.int32, x.shape, 1) < 2 * SLOT
         return jnp.where(slot, high.astype(F32), low.astype(F32)).astype(BF16)
 
+    mixes, projects, backs = {}, {}, {}
+
+    def tables(v):
+        project, back = row_matrices(v)
+        mixes[v] = by_slot(jnp.dot(back, project, precision=HIGH, preferred_element_type=F32))
+        projects[v], backs[v] = by_slot(project), split(back)
+
     def measured_along(v):
-        project, back = row_matrices(v)
-        mix = by_slot(jnp.dot(back, project, precision=HIGH, preferred_element_type=F32))
-        back_high, back_low = split(back)
+        back_high, back_low = backs[v]
         reads[v].wait()
         data_high, data_low = split(frame[v])
         both = dot(jnp.concatenate([back_high, back_low], axis=0), data_high)
         along[v] = both[:SLOT] + both[SLOT:] + dot(back_high, data_low)
-        return mix, by_slot(project)
 
     writes = [
         pltpu.make_async_copy(frame.at[v], residual.at[v], write_sem.at[v]) for v in range(views)
     ]
 
-    def subtract(v, project):
-        frame[v] = frame[v] - dot(project, stack[v])
+    def subtract(v):
+        frame[v] = frame[v] - dot(projects[v], stack[v])
         writes[v].start()
 
     def to_pair(v):
@@ -199,7 +232,7 @@
         def _():
             pass_copy(v).start()
 
-    def to_backward(v, mix):
+    def to_backward(v):
         @pl.when(has_backward)
         def _():
             pass_copy(v).wait_recv()
@@ -212,7 +245,7 @@
         stack[v, SLOT : 2 * SLOT] = low
         stack[v, 2 * SLOT : 3 * SLOT] = high
         stack[v, 3 * SLOT :] = low
-        along[v] = along[v] - dot(mix, stack[v])
+        along[v] = along[v] - dot(mixes[v], stack[v])
 
         @pl.when(has_backward)
         def _():
@@ -257,28 +290,18 @@
             return carry
 
         lax.fori_loop(0, chunks, step, 0)
-    mixes, projects = {}, {}
-
-    def prepare(v):
-        mixes[v], projects[v] = measured_along(v)
-
     def begin(v):
         spread_view(v)
+        if v == 0:
+            await_barrier()
         core_copy(v).start()
 
-    steps = (
-        begin,
-        to_pair,
-        prepare,
-        to_onward,
-        lambda v: to_backward(v, mixes[v]),
-        along_to_pair,
-        lambda v: subtract(v, projects[v]),
-        along_to_core,
-        gather_view,
-    )
-    for turn in order_of(views):
-        steps[turn[0]](turn[1])
+    steps = {
+        "b": begin, "p": to_pair, "t": tables, "o": to_onward, "m": measured_along,
+        "w": to_backward, "a": along_to_pair, "s": subtract, "c": along_to_core, "g": gather_view,
+    }
+    for step, v in ORDER:
+        steps[step](v)
 
     for v in range(views):
         core_copy(v).wait_send()
@@ -300,29 +323,8 @@
 def on_device(
     volume, measured, band_start, band_length, row_offset, row_weight, col_index, col_weight
 ):
-    slab = lax.axis_index("slab")
     depth, cells = volume.shape
     views, rows, part = measured.shape
-    taps = row_offset.shape[1]
-    start = jnp.repeat(band_start, depth, axis=1)[:, None, :]
-    length = jnp.repeat(band_length, depth, axis=1)[:, None, :]
-    row = (start + row_offset - slab * rows).astype(F32)
-    live = jnp.where(row_offset < length, row_weight, 0.0)
-    rest = jnp.zeros((views, 8 - 3 * taps, row.shape[2]), F32)
-    table = jnp.concatenate([row, row_weight, live, rest], axis=1)
-    table = jnp.pad(table, ((0, 0), (0, 0), (depth, depth)))
-    pair = slab + 1 - 2 * lax.rem(slab, 2)
-    table = jnp.concatenate(
-        [
-            lax.dynamic_slice_in_dim(table, (at + 1) * depth, depth, 2)
-            for at in (pair, slab, 2 * slab - pair)
-        ],
-        axis=2,
-    )
-    table = jnp.pad(table, ((0, 0), (0, 0), (0, SLOT - 3 * depth)))
-    lanes = jnp.tile(table, (1, 1, 4))
-    columns = jnp.swapaxes(table, 1, 2)
-
     vmem, dma = pltpu.VMEM, pltpu.SemaphoreType.DMA
     in_vmem, anywhere = pl.BlockSpec(memory_space=pltpu.VMEM), pl.BlockSpec(memory_space=pl.ANY)
     groups = 2 * part // LOW
@@ -332,7 +334,8 @@
             jax.ShapeDtypeStruct(measured.shape, F32),
             jax.ShapeDtypeStruct(volume.shape, F32),
         ),
-        in_specs=[in_vmem] * 5 + [anywhere],
+        in_specs=[in_vmem] * 5 + [pl.BlockSpec(memory_space=pltpu.SMEM)] * 2
+        + [pl.BlockSpec(memory_space=pltpu.HBM)],
         out_specs=(anywhere, in_vmem),
         scratch_shapes=[
             vmem((views, LOW, cells), BF16),
@@ -357,7 +360,7 @@
         compiler_params=pltpu.CompilerParams(
             collective_id=0, has_side_effects=True, vmem_limit_bytes=56 * 1024 * 1024
         ),
-    )(volume, col_index, col_weight, lanes, columns, measured)
+    )(volume, col_index, col_weight, row_offset, row_weight, band_start, band_length, measured)
 
 
 def solution(mesh):

time: 51.1 us -> 42.2 us (0.83)
  local copies, waits for them, and re-layouts: 8.9 us -> 5.59 us
  Pallas kernels: 38.9 us -> 35.7 us
  other arithmetic: 2.26 us -> 0 us
    pallas_call x1, Pallas kernels: 38.9 us -> 35.7 us  [on_device(): pl.pallas_call(kernel, out_shape=(jax.ShapeDtypeStruct(measured.shape, F3...]
    broadcast_in_dim x3 -> x0, local copies, waits for them, and re-layouts: 1.5 us -> none  [the longest x1 0.75 us: on_device(): start = jnp.repeat(band_start, depth, axis=1)[:, None, :]]
    concatenate x2 -> x0, other arithmetic: 0.85 us -> none  [the longest x1 0.78 us: on_device(): table = jnp.concatenate([row, row_weight, live, rest], axis=1)]
    another operation x2 -> x0, local copies, waits for them, and re-layouts: 0.72 us -> none  [on_device(): lanes = jnp.tile(table, (1, 1, 4))]
    select_n x1 -> x0, other arithmetic: 0.71 us -> none  [on_device(): live = jnp.where(row_offset < length, row_weight, 0.0)]
    convert_element_type x1 -> x0, other arithmetic: 0.69 us -> none  [on_device(): row = (start + row_offset - slab * rows).astype(F32)]
    transpose x1 -> x0, local copies, waits for them, and re-layouts: 0.67 us -> none  [on_device(): columns = jnp.swapaxes(table, 1, 2)]
    unnamed x5 -> x4, local copies, waits for them, and re-layouts: 5.66 us -> 5.59 us
where the time goes in v3:
time: 42.2 us; the launch traced here: 41.9 us
  Pallas kernels  35.7 us (85%)
  local copies, waits for them, and re-layouts  5.59 us (13%)
  between operations  0.65 us (2%)
    pallas_call x1, Pallas kernels, on_device(): pl.pallas_call(kernel, out_shape=(jax.ShapeDtypeStruct(measured.shape, F3...  35.7 us
    unnamed x4, local copies, waits for them, and re-layouts  5.59 us

profile of v3, /device:TPU:0, one launch (start us, length us, event | category | flops | bytes accessed | tf_op | source)
XLA Modules:
  0.0 41.9 jit_solution(1939370793544992143)
XLA Ops:
  0.6 35.7 %shard_map.95 = (f32[3,256,1536]{2,1,0:T(8,128)}, f32[16,4096]{1,0:T(8,128)}) custom-call(f32[16,4096]{1,0:T(8,128)} %volume.1, s32[3,2,8192]{2,1,0:T(2,128)} %col_index.1, f32[3,2,8192]{2,1,0:T(2,128)} %col_weight.1, s32[3,2,128]{2,1,0:T(2,128)} %row_offset.1, f32[3,2,128]{2,1,0:T(2,128)} %row_weight.1, s32[3,8]{1,0:T(4,128)} %band_start.1, ...), custom_call_target="tpu_custom_call" | custom-call | tf_op jit(solution)/shard_map/pallas_call | solution.py:331
  36.3 0.0 copy-start
  36.3 4.9 %copy.12 = f32[3,256,1536]{2,1,0:T(8,128)} copy(f32[3,256,1536]{2,1,0:T(8,128)} %get-tuple-element.4) | data formatting | bytes 9437184
  41.2 0.0 copy-done
  41.2 0.7 %copy.13 = f32[16,4096]{1,0:T(8,128)} copy(f32[16,4096]{1,0:T(8,128)S(1)} %copy-done) | data formatting | bytes 524288
Async XLA Ops:
  36.3 4.9 %copy-start = (f32[16,4096]{1,0:T(8,128)S(1)}, f32[16,4096]{1,0:T(8,128)}, u32[]{:S(2)}) copy-start(f32[16,4096]{1,0:T(8,128)} %get-tuple-element.5) | copy-start | bytes 786436

commit v4 on v3

--- a/solution.py
+++ b/solution.py
@@ -95,25 +95,33 @@
             {"blk": other},
         )
 
-    def pair_copy(v):
-        return remote(
-            mine.at[v], from_pair.at[v], pair_send.at[v], pair_recv.at[v], {"slab": pair}
-        )
-
-    def pass_copy(v):
-        return remote(
-            from_pair.at[v], from_far.at[v], pass_send.at[v], pass_recv.at[v], {"slab": onward}
-        )
-
-    def far_copy(v):
-        return remote(
-            along.at[v, pl.ds(2 * depth, depth)], far_in.at[v], far_send.at[v], far_recv.at[v],
-            {"slab": backward},
-        )
-
-    def near_copy(v):
-        return remote(
-            pair_out.at[v], pair_in.at[v], near_send.at[v], near_recv.at[v], {"slab": pair}
+    half = part // 2
+
+    def cols(n):
+        return pl.ds(half * n, half)
+
+    def pair_copy(v, n):
+        return remote(
+            mine.at[v, :, cols(n)], from_pair.at[v, :, cols(n)], pair_send.at[v, n],
+            pair_recv.at[v, n], {"slab": pair},
+        )
+
+    def pass_copy(v, n):
+        return remote(
+            from_pair.at[v, :, cols(n)], from_far.at[v, :, cols(n)], pass_send.at[v, n],
+            pass_recv.at[v, n], {"slab": onward},
+        )
+
+    def far_copy(v, n):
+        return remote(
+            along.at[v, pl.ds(2 * depth, depth), cols(n)], far_in.at[v, :, cols(n)],
+            far_send.at[v, n], far_recv.at[v, n], {"slab": backward},
+        )
+
+    def near_copy(v, n):
+        return remote(
+            pair_out.at[v, :, cols(n)], pair_in.at[v, :, cols(n)], near_send.at[v, n],
+            near_recv.at[v, n], {"slab": pair},
         )
 
     def last_copy(v):
@@ -223,44 +231,53 @@
     def to_pair(v):
         core_copy(v).wait_recv()
         mine[v] = spread[v, :, my_cols] + from_core[v]
-        pair_copy(v).start()
+        for n in range(2):
+            pair_copy(v, n).start()
 
     def to_onward(v):
-        pair_copy(v).wait_recv()
-
-        @pl.when(has_onward)
-        def _():
-            pass_copy(v).start()
+        for n in range(2):
+            pair_copy(v, n).wait_recv()
+
+            @pl.when(has_onward)
+            def _(n=n):
+                pass_copy(v, n).start()
 
     def to_backward(v):
-        @pl.when(has_backward)
-        def _():
-            pass_copy(v).wait_recv()
-
-        slices = jnp.concatenate(
-            [from_pair[v], mine[v], from_far[v], jnp.zeros((SLOT - 3 * depth, part), F32)], axis=0
-        )
-        high, low = split(slices)
-        stack[v, 0:SLOT] = high
-        stack[v, SLOT : 2 * SLOT] = low
-        stack[v, 2 * SLOT : 3 * SLOT] = high
-        stack[v, 3 * SLOT :] = low
-        along[v] = along[v] - dot(mixes[v], stack[v])
-
-        @pl.when(has_backward)
-        def _():
-            far_copy(v).start()
+        for n in range(2):
+
+            @pl.when(has_backward)
+            def _(n=n):
+                pass_copy(v, n).wait_recv()
+
+            slices = jnp.concatenate(
+                [
+                    from_pair[v, :, cols(n)], mine[v, :, cols(n)], from_far[v, :, cols(n)],
+                    jnp.zeros((SLOT - 3 * depth, half), F32),
+                ],
+                axis=0,
+            )
+            high, low = split(slices)
+            for place, x in enumerate((high, low, high, low)):
+                stack[v, SLOT * place : SLOT * (place + 1), cols(n)] = x
+            along[v, :, cols(n)] = along[v, :, cols(n)] - dot(mixes[v], stack[v, :, cols(n)])
+
+            @pl.when(has_backward)
+            def _(n=n):
+                far_copy(v, n).start()
 
     def along_to_pair(v):
-        @pl.when(has_onward)
-        def _():
-            far_copy(v).wait_recv()
-
-        pair_out[v] = along[v, 0:depth] + far_in[v]
-        near_copy(v).start()
+        for n in range(2):
+
+            @pl.when(has_onward)
+            def _(n=n):
+                far_copy(v, n).wait_recv()
+
+            pair_out[v, :, cols(n)] = along[v, 0:depth, cols(n)] + far_in[v, :, cols(n)]
+            near_copy(v, n).start()
 
     def along_to_core(v):
-        near_copy(v).wait_recv()
+        for n in range(2):
+            near_copy(v, n).wait_recv()
         along_sum[v] = along[v, depth : 2 * depth] + pair_in[v]
         last_copy(v).start()
 
@@ -305,17 +322,18 @@
 
     for v in range(views):
         core_copy(v).wait_send()
-        pair_copy(v).wait_send()
-        near_copy(v).wait_send()
         last_copy(v).wait_send()
-
-        @pl.when(has_onward)
-        def _():
-            pass_copy(v).wait_send()
-
-        @pl.when(has_backward)
-        def _():
-            far_copy(v).wait_send()
+        for n in range(2):
+            pair_copy(v, n).wait_send()
+            near_copy(v, n).wait_send()
+
+            @pl.when(has_onward)
+            def _(n=n):
+                pass_copy(v, n).wait_send()
+
+            @pl.when(has_backward)
+            def _(n=n):
+                far_copy(v, n).wait_send()
 
         writes[v].wait()
 
@@ -356,7 +374,9 @@
             vmem((views, depth, part), F32),
             vmem((2, 2, depth * groups, LOW), BF16),
         ]
-        + [dma((views,))] * 14,
+        + [dma((views,))] * 2
+        + [dma((views, 2))] * 8
+        + [dma((views,))] * 4,
         compiler_params=pltpu.CompilerParams(
             collective_id=0, has_side_effects=True, vmem_limit_bytes=56 * 1024 * 1024
         ),

time: 42.2 us -> 42 us (level)
  no operation moved by 1% of the time
where the time goes in v4:
time: 42 us; the launch traced here: 41.9 us
  Pallas kernels  35.6 us (85%)
  local copies, waits for them, and re-layouts  5.59 us (13%)
  between operations  0.65 us (2%)
    pallas_call x1, Pallas kernels, on_device(): pl.pallas_call(kernel, out_shape=(jax.ShapeDtypeStruct(measured.shape, F3...  35.6 us
    unnamed x4, local copies, waits for them, and re-layouts  5.59 us

profile of v4, /device:TPU:0, one launch (start us, length us, event | category | flops | bytes accessed | tf_op | source)
XLA Modules:
  0.0 41.9 jit_solution(8642353563854614346)
XLA Ops:
  0.6 35.6 %shard_map.95 = (f32[3,256,1536]{2,1,0:T(8,128)}, f32[16,4096]{1,0:T(8,128)}) custom-call(f32[16,4096]{1,0:T(8,128)} %volume.1, s32[3,2,8192]{2,1,0:T(2,128)} %col_index.1, f32[3,2,8192]{2,1,0:T(2,128)} %col_weight.1, s32[3,2,128]{2,1,0:T(2,128)} %row_offset.1, f32[3,2,128]{2,1,0:T(2,128)} %row_weight.1, s32[3,8]{1,0:T(4,128)} %band_start.1, ...), custom_call_target="tpu_custom_call" | custom-call | tf_op jit(solution)/shard_map/pallas_call | solution.py:349
  36.3 0.0 copy-start
  36.3 4.9 %copy.12 = f32[3,256,1536]{2,1,0:T(8,128)} copy(f32[3,256,1536]{2,1,0:T(8,128)} %get-tuple-element.4) | data formatting | bytes 9437184
  41.2 0.0 copy-done
  41.2 0.7 %copy.13 = f32[16,4096]{1,0:T(8,128)} copy(f32[16,4096]{1,0:T(8,128)S(1)} %copy-done) | data formatting | bytes 524288
Async XLA Ops:
  36.3 4.9 %copy-start = (f32[16,4096]{1,0:T(8,128)S(1)}, f32[16,4096]{1,0:T(8,128)}, u32[]{:S(2)}) copy-start(f32[16,4096]{1,0:T(8,128)} %get-tuple-element.5) | copy-start | bytes 786436
